TPU v7x, 32 devices: a whole 2x2x4 slice. The times are simulated.
32 devices in a mesh: tm: 4 (over y, x), space: 8 (over z, core).
Axes of the slice: x: 2, y: 2, z: 4, core: 2. Of those that a mesh axis runs over, the one named last changes fastest.
Arguments:
- q_start: float32 [5, 32, 64, 128], P(None, 'space'), may hold values from -3.6 to 3.6
- guess: float32 [4, 5, 32, 64, 128], P('tm', None, 'space'), may hold values from -3.6 to 3.6
Outputs:
- corrected: float32 [4, 5, 32, 64, 128], P('tm', None, 'space')
- residual: float32 [4, 5, 32, 64, 128], P('tm', None, 'space')
All inputs are finite; a program needn't handle non-finite values.
Results may differ from a plain program's by a relative error of at most 0.00011.
Values sent between devices are 32-bit elements; how exact they have to be, the bound alone decides.
A program may use at most 64 MiB of HBM per device.

v0:
```python
import jax
import jax.numpy as jnp
from jax import lax
from jax.sharding import PartitionSpec as P

NZ = 128
COMP = 5
STEPS_SLAB = 2
SWEEPS = 2
BLK = 4


time_step = 0.1
cross = 8.0
axial = 2.0
linear_rate = 0.1
quadratic_rate = 0.5
cubic_rate = 1.0


def with_halo(block, sides, width):
    for axis, dim in sides:
        count = lax.axis_size(axis)
        forward = [(i, i + 1) for i in range(count - 1)]
        backward = [(target, source) for source, target in forward]
        low = lax.ppermute(
            lax.slice_in_dim(block, block.shape[dim] - width, None, axis=dim), axis, forward
        )
        high = lax.ppermute(lax.slice_in_dim(block, 0, width, axis=dim), axis, backward)
        block = jnp.concatenate([low, block, high], axis=dim)
    return block


def passed_along(block, axis, distance):
    devices = range(lax.axis_size(axis))
    route = [(i - distance, i) for i in devices if i - distance in devices]
    return lax.ppermute(block, axis, route)


def prefix(part, axis, combine, identity):
    place = lax.axis_index(axis)
    gathered = jax.tree.map(lambda a: lax.all_gather(a, axis), part)
    state = jax.tree.map(lambda a, e: jnp.zeros_like(a) + jnp.asarray(e, a.dtype), part, identity)

    def one(turn, state):
        return combine(
            state, jax.tree.map(lambda a: lax.dynamic_index_in_dim(a, turn, 0, False), gathered)
        )

    return lax.fori_loop(0, place, one, state)


def bulk_terms(field):
    first, second, third, fourth, fifth = (field[0], field[1], field[2], field[3], field[4])
    sixth = -first - fourth
    s_aa = first * first + second * second + third * third
    s_ab = first * second + second * fourth + third * fifth
    s_ac = first * third + second * fifth + third * sixth
    s_bb = second * second + fourth * fourth + fifth * fifth
    s_bc = second * third + fourth * fifth + fifth * sixth
    trace = (
        first * first
        + fourth * fourth
        + sixth * sixth
        + 2.0 * (second * second + third * third + fifth * fifth)
    )
    quad = jnp.stack([s_aa - trace / 3.0, s_ab, s_ac, s_bb - trace / 3.0, s_bc])
    source = field + time_step * quadratic_rate * quad
    diagonal = 1.0 + time_step * (linear_rate + cubic_rate * trace) + 2.0 * (2.0 * cross + axial)
    return (source, diagonal)


def jacobi(extended, source, diagonal):
    inner = extended[:, 1:-1]
    along_x = extended[:, :-2] + extended[:, 2:]
    padded_y = jnp.pad(inner, ((0, 0), (0, 0), (1, 1), (0, 0)))
    along_y = padded_y[:, :, :-2] + padded_y[:, :, 2:]
    along_z = jnp.roll(inner, 1, 3) + jnp.roll(inner, -1, 3)
    return (source + cross * (along_x + along_y) + axial * along_z) / diagonal[None]


def inside_rows(margin, rows):
    device = lax.axis_index("space")
    row_coord = device * rows - margin + jnp.arange(rows + 2 * margin, dtype=jnp.int32)
    row_inside = (row_coord >= 0) & (row_coord < rows * lax.axis_size("space"))
    return jnp.where(row_inside, 1.0, 0.0).astype(jnp.float32)


def extend(field, margin):
    return with_halo(field, (("space", 1),), margin)


def advance(extended, steps, inside):
    done = 0
    for step in range(steps):
        source, diagonal = bulk_terms(extended)
        current = extended
        for sweep in range(SWEEPS):
            offset = sweep + 1
            rows = current.shape[1] - 2
            done = done + 1
            source_part = source[:, offset : offset + rows]
            diagonal_part = diagonal[offset : offset + rows]
            current = jacobi(current, source_part, diagonal_part)
            current = current * inside[done : done + rows][None, :, None, None]
        extended = current
    return extended


def propagate(field):
    reach = STEPS_SLAB * SWEEPS
    inside = inside_rows(reach, field.shape[1])
    field = advance(extend(field, reach), STEPS_SLAB, inside)
    return field


def chain_combine(earlier, later):
    return (earlier[0] * later[0], later[0] * earlier[1] + later[1])


def per_device(q_start, guess):
    own = guess[0]
    position = lax.axis_index("tm")
    prior = passed_along(own, "tm", 1)
    start = jnp.where(position == 0, q_start, prior)
    relaxed = propagate(start)
    moved = passed_along(relaxed, "tm", 1)
    start_two = jnp.where(position == 0, q_start, moved)
    again = propagate(start_two)
    residual = again - relaxed
    change = again - own
    cells_total = change.shape[1] * change.shape[2] * lax.axis_size("space")
    partial_sum = jnp.sum(change, axis=(1, 2))
    partial_sum = partial_sum.reshape(COMP, NZ // BLK, BLK).sum(axis=2)
    totals = lax.psum(partial_sum, "space")
    coarse = totals / (cells_total * BLK)
    decay = 1.0 / (1.0 + STEPS_SLAB * time_step * linear_rate)
    factor = jnp.full((), decay, jnp.float32)
    identity = (jnp.ones((), jnp.float32), jnp.zeros_like(coarse))
    passed = prefix((factor, coarse), "tm", chain_combine, identity)
    error = decay * passed[1] + coarse
    spread = jnp.broadcast_to(error[:, None, None, :, None], (COMP, 1, 1, NZ // BLK, BLK))
    spread = spread.reshape(COMP, 1, 1, NZ)
    corrected = relaxed + spread
    return (corrected[None], residual[None])


def solution(mesh):
    return jax.shard_map(
        per_device,
        mesh=mesh,
        in_specs=(P(None, "space", None, None), P("tm", None, "space", None, None)),
        out_specs=(P("tm", None, "space", None, None), P("tm", None, "space", None, None)),
        check_vma=False,
    )
```

profile of v0, /device:TPU:0, one launch (start us, length us, event | category | flops | bytes accessed | tf_op | source)
XLA Modules:
  0.0 116.1 jit_solution(2148453972809193271)
XLA Ops:
  0.6 4.9 %collective-permute-start = (f32[5,4,64,128]{3,2,1,0:T(8,128)}, f32[5,4,64,128]{3,2,1,0:T(8,128)S(1)}, u32[]{:S(2)}, u32[]{:S(2)}) collective-permute-start(f32[5,4,64,128]{3,2,1,0:T(8,128)} %bitcast.32), channel_id=1, source_target_pairs={{0,8},{8,16},{16,24},{1,9},{9,17},{17,25},{2,10},{10,18},{18,26},{... | collective-permute-start | bytes 1966088 | tf_op jit(solution)/shard_map/ppermute | solution.py:37
  5.5 14.2 %collective-permute-done = f32[5,4,64,128]{3,2,1,0:T(8,128)S(1)} collective-permute-done((f32[5,4,64,128]{3,2,1,0:T(8,128)}, f32[5,4,64,128]{3,2,1,0:T(8,128)S(1)}, u32[]{:S(2)}, u32[]{:S(2)}) %collective-permute-start) | collective-permute-done | bytes 655392 | tf_op jit(solution)/shard_map/ppermute | solution.py:37
  19.8 1.2 %broadcast_select_fusion.1 = f32[5,4,64,128]{3,2,1,0:T(8,128)S(1)} fusion(f32[5,4,64,128]{3,2,1,0:T(8,128)} %param.4, f32[5,4,64,128]{3,2,1,0:T(8,128)S(1)} %collective-permute-done, pred[]{:T(512)S(6)} %eq.4), kind=kLoop, calls=%fused_computation.127 | loop fusion | flops 163840 | bytes 1966081 | tf_op jit(solution)/shard_map/jit(_where)/select_n | solution.py:125
  20.9 1.3 %collective-permute-start.2 = (f32[5,4,64,128]{3,2,1,0:T(8,128)S(1)}, f32[5,4,64,128]{3,2,1,0:T(8,128)S(1)}, u32[]{:S(2)}, u32[]{:S(2)}) collective-permute-start(f32[5,4,64,128]{3,2,1,0:T(8,128)S(1)} %broadcast_select_fusion.1), channel_id=1, source_target_pairs={{1,0},{2,1},{3,2},{4,3},{5,4},{6,5},{7,6},{9,8},{10,9},{11,10},{12... | collective-permute-start | bytes 1966088 | tf_op jit(solution)/shard_map/ppermute | solution.py:29
  22.2 3.1 %collective-permute-start.1 = (f32[5,4,64,128]{3,2,1,0:T(8,128)S(1)}, f32[5,4,64,128]{3,2,1,0:T(8,128)S(1)}, u32[]{:S(2)}, u32[]{:S(2)}) collective-permute-start(f32[5,4,64,128]{3,2,1,0:T(8,128)S(1)} %broadcast_select_fusion.1), channel_id=1, source_target_pairs={{0,1},{1,2},{2,3},{3,4},{4,5},{5,6},{6,7},{8,9},{9,10},{10,11},{11... | collective-permute-start | bytes 1966088 | tf_op jit(solution)/shard_map/ppermute | solution.py:26
  25.6 1.4 %collective-permute-done.1 = f32[5,4,64,128]{3,2,1,0:T(8,128)S(1)} collective-permute-done((f32[5,4,64,128]{3,2,1,0:T(8,128)S(1)}, f32[5,4,64,128]{3,2,1,0:T(8,128)S(1)}, u32[]{:S(2)}, u32[]{:S(2)}) %collective-permute-start.1) | collective-permute-done | bytes 655392 | tf_op jit(solution)/shard_map/ppermute | solution.py:26
  27.5 0.6 fusion.71
  28.2 0.6 fusion.72
  30.0 1.1 copy-done.3
  31.1 0.5 slice-done.1
  31.6 1.7 %fusion.15 = f32[5,10,64,128]{3,2,1,0:T(8,128)S(1)} fusion(f32[5,10,64,1]{3,2,1,0:T(8,128)S(1)} %get-tuple-element.72, f32[5,10,64,127]{3,2,1,0:T(8,128)S(1)} %get-tuple-element.74, f32[5,10,64,127]{3,2,1,0:T(8,128)S(1)} %get-tuple-element.73, f32[5,10,64,1]{3,2,1,0:T(8,128)S(1)} %get-tuple-element.71, f32[5,10,64,128]{3,2,1,0:T(8,128)S(1)} %slice-done.1, ...), kind=kLoop, calls=%fused_computation.28 | loop fusion | flops 4915200 | bytes 11796520 | tf_op jit(solution)/shard_map/mul | solution.py:105
  34.3 1.2 %fusion.31 = f32[5,8,64,128]{3,2,1,0:T(8,128)S(1)} fusion(f32[5,8,64,1]{3,2,1,0:T(8,128)S(1)} %get-tuple-element.80, f32[5,8,64,127]{3,2,1,0:T(8,128)S(1)} %get-tuple-element.82, f32[5,8,64,127]{3,2,1,0:T(8,128)S(1)} %get-tuple-element.81, f32[5,8,64,1]{3,2,1,0:T(8,128)S(1)} %get-tuple-element.79, f32[5,8,64,128]{3,2,1,0:T(8,128)S(1)} %slice.525, ...), kind=kLoop, calls=%fused_computation.54 | loop fusion | flops 3932160 | bytes 9437216 | tf_op jit(solution)/shard_map/mul | solution.py:105
  37.2 0.9 fusion.47
  38.7 0.7 fusion.63
  39.4 3.2 %collective-permute-start.3 = (f32[5,4,64,128]{3,2,1,0:T(8,128)S(1)}, f32[5,4,64,128]{3,2,1,0:T(8,128)S(1)}, u32[]{:S(2)}, u32[]{:S(2)}) collective-permute-start(f32[5,4,64,128]{3,2,1,0:T(8,128)S(1)} %fusion.63), channel_id=1, source_target_pairs={{0,8},{8,16},{16,24},{1,9},{9,17},{17,25},{2,10},{10,18},{18,26},{... | collective-permute-start | bytes 1966088 | tf_op jit(solution)/shard_map/ppermute | solution.py:37
  42.6 9.0 %collective-permute-done.3 = f32[5,4,64,128]{3,2,1,0:T(8,128)S(1)} collective-permute-done((f32[5,4,64,128]{3,2,1,0:T(8,128)S(1)}, f32[5,4,64,128]{3,2,1,0:T(8,128)S(1)}, u32[]{:S(2)}, u32[]{:S(2)}) %collective-permute-start.3) | collective-permute-done | bytes 655392 | tf_op jit(solution)/shard_map/ppermute | solution.py:37
  51.7 1.3 %collective-permute-start.5 = (f32[5,4,64,128]{3,2,1,0:T(8,128)S(1)}, f32[5,4,64,128]{3,2,1,0:T(8,128)S(1)}, u32[]{:S(2)}, u32[]{:S(2)}) collective-permute-start(f32[5,4,64,128]{3,2,1,0:T(8,128)S(1)} %broadcast_select_fusion), channel_id=1, source_target_pairs={{1,0},{2,1},{3,2},{4,3},{5,4},{6,5},{7,6},{9,8},{10,9},{11,10},{12... | collective-permute-start | bytes 1966088 | tf_op jit(solution)/shard_map/ppermute | solution.py:29
  53.0 8.8 %collective-permute-start.4 = (f32[5,4,64,128]{3,2,1,0:T(8,128)S(1)}, f32[5,4,64,128]{3,2,1,0:T(8,128)S(1)}, u32[]{:S(2)}, u32[]{:S(2)}) collective-permute-start(f32[5,4,64,128]{3,2,1,0:T(8,128)S(1)} %broadcast_select_fusion), channel_id=1, source_target_pairs={{0,1},{1,2},{2,3},{3,4},{4,5},{5,6},{6,7},{8,9},{9,10},{10,11},{11... | collective-permute-start | bytes 1966088 | tf_op jit(solution)/shard_map/ppermute | solution.py:26
  61.8 0.6 dynamic-slice
  62.4 0.8 dynamic-update-slice
  63.1 10.8 %all-reduce.8 = f32[4]{0:T(128)S(1)} all-reduce(f32[4]{0:T(128)S(1)} %dynamic-update-slice), channel_id=1, replica_groups=mesh['tm'=4,'space'=8] {'tm'}, use_global_device_ids=true, to_apply=%add.8 | all-reduce | flops 4 | bytes 32
  74.5 0.6 fusion.69
  75.1 0.6 fusion.70
  76.9 1.1 copy-done.1
  78.0 0.5 slice-done
  78.5 1.7 %fusion.14 = f32[5,10,64,128]{3,2,1,0:T(8,128)S(1)} fusion(f32[5,10,64,1]{3,2,1,0:T(8,128)S(1)} %get-tuple-element.68, f32[5,10,64,127]{3,2,1,0:T(8,128)S(1)} %get-tuple-element.70, f32[5,10,64,127]{3,2,1,0:T(8,128)S(1)} %get-tuple-element.69, f32[5,10,64,1]{3,2,1,0:T(8,128)S(1)} %get-tuple-element.67, f32[5,10,64,128]{3,2,1,0:T(8,128)S(1)} %slice-done, ...), kind=kLoop, calls=%fused_computation.27 | loop fusion | flops 4915200 | bytes 11796520 | tf_op jit(solution)/shard_map/mul | solution.py:105
  81.3 1.2 %fusion.30 = f32[5,8,64,128]{3,2,1,0:T(8,128)S(1)} fusion(f32[5,8,64,1]{3,2,1,0:T(8,128)S(1)} %get-tuple-element.76, f32[5,8,64,127]{3,2,1,0:T(8,128)S(1)} %get-tuple-element.78, f32[5,8,64,127]{3,2,1,0:T(8,128)S(1)} %get-tuple-element.77, f32[5,8,64,1]{3,2,1,0:T(8,128)S(1)} %get-tuple-element.75, f32[5,8,64,128]{3,2,1,0:T(8,128)S(1)} %slice.571, ...), kind=kLoop, calls=%fused_computation.53 | loop fusion | flops 3932160 | bytes 9437216 | tf_op jit(solution)/shard_map/mul | solution.py:105
  84.2 0.9 fusion.46
  85.6 1.5 %subtract_bitcast_fusion = (f32[1,5,4,64,128]{4,3,2,1,0:T(8,128)}, f32[5,4,64,128]{3,2,1,0:T(8,128)S(1)}) fusion(f32[5,4,64,128]{3,2,1,0:T(8,128)S(1)} %fusion.63, f32[4]{0:T(128)S(1)} %slice.445, f32[4,64,128]{2,1,0:T(8,128)S(1)} %slice_bitcast_fusion.6, f32[5,4,64,1]{3,2,1,0:T(8,128)S(1)} %get-tuple-element.92, ...), kind=kLoop, calls=%fused_computation.101 | loop fusion | flops 2129920 | bytes 6029328 | tf_op jit(solution)/shard_map/broadcast_in_dim | solution.py:145
  87.5 19.4 %psum.7 = f32[5,32]{1,0:T(8,128)S(1)} all-reduce(f32[5,32]{1,0:T(8,128)S(1)} %reduce_sum.19), channel_id=1, replica_groups=mesh['tm'=4,'space'=8] {'space'}, use_global_device_ids=true, to_apply=%region_2.3 | all-reduce | flops 160 | bytes 1280 | tf_op jit(solution)/shard_map/psum | solution.py:135
  106.9 8.1 %all-gather.1 = f32[4,5,32]{2,1,0:T(8,128)S(1)} all-gather(f32[1,5,32]{2,1,0:T(8,128)S(1)} %multiply_bitcast_fusion), channel_id=2, replica_groups=mesh['tm'=4,'space'=8] {'tm'}, dimensions={0}, use_global_device_ids=true | all-gather | bytes 3200 | tf_op jit(solution)/shard_map/all_gather | solution.py:42
  115.2 0.9 add_bitcast_fusion
  (89 shorter events, 10.5 us)
Async XLA Ops:
  0.6 19.1 %collective-permute-start = (f32[5,4,64,128]{3,2,1,0:T(8,128)}, f32[5,4,64,128]{3,2,1,0:T(8,128)S(1)}, u32[]{:S(2)}, u32[]{:S(2)}) collective-permute-start(f32[5,4,64,128]{3,2,1,0:T(8,128)} %bitcast.32), channel_id=1, source_target_pairs={{0,8},{8,16},{16,24},{1,9},{9,17},{17,25},{2,10},{10,18},{18,26},{... | collective-permute-start | bytes 1966088 | tf_op jit(solution)/shard_map/ppermute | solution.py:37
  20.9 4.7 %collective-permute-start.2 = (f32[5,4,64,128]{3,2,1,0:T(8,128)S(1)}, f32[5,4,64,128]{3,2,1,0:T(8,128)S(1)}, u32[]{:S(2)}, u32[]{:S(2)}) collective-permute-start(f32[5,4,64,128]{3,2,1,0:T(8,128)S(1)} %broadcast_select_fusion.1), channel_id=1, source_target_pairs={{1,0},{2,1},{3,2},{4,3},{5,4},{6,5},{7,6},{9,8},{10,9},{11,10},{12... | collective-permute-start | bytes 1966088 | tf_op jit(solution)/shard_map/ppermute | solution.py:29
  22.2 4.7 %collective-permute-start.1 = (f32[5,4,64,128]{3,2,1,0:T(8,128)S(1)}, f32[5,4,64,128]{3,2,1,0:T(8,128)S(1)}, u32[]{:S(2)}, u32[]{:S(2)}) collective-permute-start(f32[5,4,64,128]{3,2,1,0:T(8,128)S(1)} %broadcast_select_fusion.1), channel_id=1, source_target_pairs={{0,1},{1,2},{2,3},{3,4},{4,5},{5,6},{6,7},{8,9},{9,10},{10,11},{11... | collective-permute-start | bytes 1966088 | tf_op jit(solution)/shard_map/ppermute | solution.py:26
  27.2 2.2 %copy-start.2 = (f32[5,12,64,128]{3,2,1,0:T(8,128)}, f32[5,12,64,128]{3,2,1,0:T(8,128)S(1)}, u32[]{:S(2)}) copy-start(f32[5,12,64,128]{3,2,1,0:T(8,128)S(1)} %pad_maximum_fusion) | copy-start | bytes 5898244
  29.6 1.5 %copy-start.3 = (f32[5,12,64,128]{3,2,1,0:T(8,128)S(1)}, f32[5,12,64,128]{3,2,1,0:T(8,128)}, u32[]{:S(2)}) copy-start(f32[5,12,64,128]{3,2,1,0:T(8,128)} %copy-done.2) | copy-start | bytes 5898244
  29.6 2.0 %slice-start.1 = ((f32[5,12,64,128]{3,2,1,0:T(8,128)}), f32[5,10,64,128]{3,2,1,0:T(8,128)S(1)}, s32[]{:S(2)}) async-start(f32[5,12,64,128]{3,2,1,0:T(8,128)} %copy-done.2), calls=%async_computation.1 | async-start | bytes 3276800 | tf_op jit(solution)/shard_map/slice | solution.py:74
  38.7 12.9 %copy-start.4 = (f32[5,4,64,128]{3,2,1,0:T(8,128)S(1)}, f32[5,4,64,128]{3,2,1,0:T(8,128)}, u32[]{:S(2)}) copy-start(f32[5,4,64,128]{3,2,1,0:T(8,128)} %param.4) | copy-start | bytes 1966084
  39.4 22.4 %copy-start.6 = (u32[32]{0:T(128)S(1)}, u32[32]{0:T(128)}, u32[]{:S(2)}) copy-start(u32[32]{0:T(128)} %constant.99) | copy-start | bytes 388
  39.4 12.2 %collective-permute-start.3 = (f32[5,4,64,128]{3,2,1,0:T(8,128)S(1)}, f32[5,4,64,128]{3,2,1,0:T(8,128)S(1)}, u32[]{:S(2)}, u32[]{:S(2)}) collective-permute-start(f32[5,4,64,128]{3,2,1,0:T(8,128)S(1)} %fusion.63), channel_id=1, source_target_pairs={{0,8},{8,16},{16,24},{1,9},{9,17},{17,25},{2,10},{10,18},{18,26},{... | collective-permute-start | bytes 1966088 | tf_op jit(solution)/shard_map/ppermute | solution.py:37
  51.7 22.2 %collective-permute-start.5 = (f32[5,4,64,128]{3,2,1,0:T(8,128)S(1)}, f32[5,4,64,128]{3,2,1,0:T(8,128)S(1)}, u32[]{:S(2)}, u32[]{:S(2)}) collective-permute-start(f32[5,4,64,128]{3,2,1,0:T(8,128)S(1)} %broadcast_select_fusion), channel_id=1, source_target_pairs={{1,0},{2,1},{3,2},{4,3},{5,4},{6,5},{7,6},{9,8},{10,9},{11,10},{12... | collective-permute-start | bytes 1966088 | tf_op jit(solution)/shard_map/ppermute | solution.py:29
  53.0 20.9 %collective-permute-start.4 = (f32[5,4,64,128]{3,2,1,0:T(8,128)S(1)}, f32[5,4,64,128]{3,2,1,0:T(8,128)S(1)}, u32[]{:S(2)}, u32[]{:S(2)}) collective-permute-start(f32[5,4,64,128]{3,2,1,0:T(8,128)S(1)} %broadcast_select_fusion), channel_id=1, source_target_pairs={{0,1},{1,2},{2,3},{3,4},{4,5},{5,6},{6,7},{8,9},{9,10},{10,11},{11... | collective-permute-start | bytes 1966088 | tf_op jit(solution)/shard_map/ppermute | solution.py:26
  74.1 2.2 %copy-start = (f32[5,12,64,128]{3,2,1,0:T(8,128)}, f32[5,12,64,128]{3,2,1,0:T(8,128)S(1)}, u32[]{:S(2)}) copy-start(f32[5,12,64,128]{3,2,1,0:T(8,128)S(1)} %pad_maximum_fusion.1) | copy-start | bytes 5898244
  76.5 1.5 %copy-start.1 = (f32[5,12,64,128]{3,2,1,0:T(8,128)S(1)}, f32[5,12,64,128]{3,2,1,0:T(8,128)}, u32[]{:S(2)}) copy-start(f32[5,12,64,128]{3,2,1,0:T(8,128)} %copy-done) | copy-start | bytes 5898244
  76.5 2.0 %slice-start = ((f32[5,12,64,128]{3,2,1,0:T(8,128)}), f32[5,10,64,128]{3,2,1,0:T(8,128)S(1)}, s32[]{:S(2)}) async-start(f32[5,12,64,128]{3,2,1,0:T(8,128)} %copy-done), calls=%async_computation | async-start | bytes 3276800 | tf_op jit(solution)/shard_map/slice | solution.py:74
  85.6 1.6 %copy-start.5 = (f32[1,5,4,64,128]{4,3,2,1,0:T(8,128)S(1)}, f32[1,5,4,64,128]{4,3,2,1,0:T(8,128)}, u32[]{:S(2)}) copy-start(f32[1,5,4,64,128]{4,3,2,1,0:T(8,128)} %param.5) | copy-start | bytes 1966084
where the time goes:
time: 118 us; the launch traced here: 116 us
  blocking collectives  38.3 us (32%)
  waiting for transfers between devices  24.6 us (21%)
  starting transfers between devices  22.6 us (19%)
  other arithmetic  17.1 us (14%)
  local copies, waits for them, and re-layouts  12.4 us (11%)
  between operations  1.28 us (1%)
    ppermute x2, waiting for transfers between devices, passed_along(): return lax.ppermute(block, axis, route)  23.2 us
    psum x1, blocking collectives, per_device(): totals = lax.psum(partial_sum, 'space')  19.4 us
    ppermute x2, starting transfers between devices, with_halo(): lax.ppermute(lax.slice_in_dim(block, block.shape[dim] - width, None, axis...  11.9 us
    unnamed x1, blocking collectives  10.8 us
    mul x7, other arithmetic, advance(): current = current * inside[done:done + rows][None, :, None, None]  8.34 us
    ppermute x2, starting transfers between devices, passed_along(): return lax.ppermute(block, axis, route)  8.12 us
    all_gather x1, blocking collectives, prefix(): gathered = jax.tree.map(lambda a: lax.all_gather(a, axis), part)  8.09 us
    slice x16, local copies, waits for them, and re-layouts, jacobi(): along_z = jnp.roll(inner, 1, 3) + jnp.roll(inner, -1, 3)  6.74 us
  transfers between devices with their start and end apart: 6, of which 3 were waited for; matrix products, arithmetic and copies ran while one was open for 1% of the time, Pallas kernels for 0%

commit v1 on v0

v1 whole, which is shorter than its diff:
```python
import functools

import jax
import jax.numpy as jnp
from jax import lax
from jax.experimental import pallas as pl
from jax.experimental.pallas import tpu as pltpu
from jax.sharding import PartitionSpec as P

STEPS_SLAB = 2
SWEEPS = 2
BLK = 4

time_step = 0.1
cross = 8.0
axial = 2.0
linear_rate = 0.1
quadratic_rate = 0.5
cubic_rate = 1.0

REACH = STEPS_SLAB * SWEEPS
TILE = 8
CHUNKS = 4
MESH = pl.DeviceIdType.MESH


def bulk(field):
    a, b, c, d, e = field
    f = -a - d
    aa, bb, cc, dd, ee, ff = a * a, b * b, c * c, d * d, e * e, f * f
    trace = aa + dd + ff + 2.0 * (bb + cc + ee)
    third = trace * (1.0 / 3.0)
    quad = (
        aa + bb + cc - third,
        a * b + b * d + c * e,
        a * c + b * e + c * f,
        bb + dd + ee - third,
        b * c + d * e + e * f,
    )
    source = [q + (time_step * quadratic_rate) * s for q, s in zip(field, quad)]
    constant = 1.0 + time_step * linear_rate + 2.0 * (2.0 * cross + axial)
    diagonal = constant + (time_step * cubic_rate) * trace
    return source, diagonal


def neighbours(ref, c, r, t, before, now, after, edge=False):
    along_x = before + after
    if edge:
        higher = pltpu.roll(now, TILE - 1, 0)
    else:
        higher = ref[c, r, pl.ds(TILE * t + TILE + 1, TILE), :]
    along_y = ref[c, r, pl.ds(TILE * t + TILE - 1, TILE), :] + higher
    lanes = now.shape[1]
    along_z = pltpu.roll(now, 1, 1) + pltpu.roll(now, lanes - 1, 1)
    return (cross / axial) * (along_x + along_y) + along_z


def tile_rows(ref, r, t):
    at = pl.ds(pl.multiple_of(TILE * t + TILE, TILE), TILE)
    return [ref[c, r, at, :] for c in range(ref.shape[0])]


def first_sweep(ref, out, src, inv, rows, inside, lo, hi, partial):
    comp = ref.shape[0]
    tiles = ref.shape[2] // TILE - 2

    def one(edge, t, carry):
        at = pl.ds(pl.multiple_of(TILE * t + TILE, TILE), TILE)
        before, now = tile_rows(ref, rows[0] - 1, t), tile_rows(ref, rows[0], t)
        for r in rows:
            after = tile_rows(ref, r + 1, t)
            source, diagonal = bulk(now)
            inverse = inside(r) / diagonal
            scaled = axial * inverse
            inv[r, at, :] = scaled
            for c in range(comp):
                part = source[c] * inverse
                src[c, r, at, :] = part
                out[c, r, at, :] = part + scaled * neighbours(
                    ref, c, r, t, before[c], now[c], after[c], edge
                )
            before, now = now, after
        return carry

    if not partial:
        lax.fori_loop(lo, hi, functools.partial(one, False), 0)
        return
    last = hi - 1 + lax.div(hi, tiles)
    lax.fori_loop(lo, last, functools.partial(one, False), 0)
    lax.fori_loop(last, hi, functools.partial(one, True), 0)


def next_sweep(ref, store, src, inv, rows, lo, hi):
    comp = ref.shape[0]

    def one(t, carry):
        at = pl.ds(pl.multiple_of(TILE * t + TILE, TILE), TILE)
        before, now = tile_rows(ref, rows[0] - 1, t), tile_rows(ref, rows[0], t)
        for r in rows:
            after = tile_rows(ref, r + 1, t)
            scaled = inv[r, at, :]
            for c in range(comp):
                store(c, r, t, src[c, r, at, :] + scaled * neighbours(ref, c, r, t, before[c], now[c], after[c]))
            before, now = now, after
        return carry

    lax.fori_loop(lo, hi, one, 0)


def phi(ref, out, w1, w2, src, inv, inside, rows, lo, hi, out_lo, out_hi):
    wide = rows + 2 * REACH

    def keep(c, r, t, value):
        w2[c, r, pl.ds(pl.multiple_of(TILE * t + TILE, TILE), TILE), :] = value

    def last(c, r, t, value):
        out[c, r - REACH, pl.ds(pl.multiple_of(TILE * t, TILE), TILE), :] = value

    first_sweep(ref, w1, src, inv, range(1, wide - 1), inside, lo, hi, True)
    next_sweep(w1, keep, src, inv, range(2, wide - 2), lo, hi)
    first_sweep(w2, w1, src, inv, range(3, wide - 3), inside, lo, hi, False)
    next_sweep(w1, last, src, inv, range(4, wide - 4), out_lo, out_hi)


def kernel(
    n, slabs, q_ref, g_ref, corrected_ref, residual_ref,
    e1, e2, w1, w2, src, inv, x, again, relaxed, guess, result, rest, sums, terms,
    load_sem, h1_send, h1_recv, h2_send, h2_recv, x_send, r_send, f_send, s_recv, r_recv,
    sum_send, sum_recv, term_send, term_recv, out_sem,
):
    p = lax.axis_index("tm")
    s = lax.axis_index("space")
    comp, rows, ny, nz = x.shape
    tiles = ny // TILE
    mid = pl.ds(REACH, rows)
    body = pl.ds(TILE, ny)
    has_left, has_right = s > 0, s < n - 1

    own = e1.at[:, mid, body, :]
    load_guess = pltpu.make_async_copy(g_ref.at[0], guess, load_sem.at[0])
    load_guess.start()
    own_guess = pltpu.make_async_copy(g_ref.at[0], own, load_sem.at[1])
    own_start = pltpu.make_async_copy(q_ref, own, load_sem.at[1])
    first_start = pltpu.make_async_copy(q_ref, e2.at[:, mid, body, :], load_sem.at[2])
    pl.when(p < slabs - 1)(own_guess.start)
    pl.when(p == slabs - 1)(own_start.start)
    pl.when(p == 0)(first_start.start)

    barrier = pltpu.get_barrier_semaphore()

    def greet_space(d, carry):
        pl.semaphore_signal(barrier, inc=1, device_id={"space": lax.rem(s + d, n)}, device_id_type=MESH)
        return carry

    lax.fori_loop(1, n, greet_space, 0)
    for d in range(1, slabs):
        pl.semaphore_signal(barrier, inc=1, device_id={"tm": lax.rem(p + d, slabs)}, device_id_type=MESH)

    wide = rows + 2 * REACH
    border = jnp.zeros((TILE, nz), jnp.float32)

    def clear_pads(r, carry):
        for ref in (e1, e2, w1, w2):
            for c in range(comp):
                ref[c, r, pl.ds(0, TILE), :] = border
                ref[c, r, pl.ds(TILE + ny, TILE), :] = border
        return carry

    lax.fori_loop(0, wide, clear_pads, 0)

    def clear_rows(first):
        def one(t, carry):
            at = pl.ds(pl.multiple_of(TILE * t + TILE, TILE), TILE)
            for ref in (e1, e2):
                for c in range(comp):
                    for r in range(REACH):
                        ref[c, first + r, at, :] = border
            return carry

        lax.fori_loop(0, tiles, one, 0)

    pl.when(s == 0)(functools.partial(clear_rows, 0))
    pl.when(s == n - 1)(functools.partial(clear_rows, REACH + rows))

    left_inside = jnp.where(has_left, 1.0, 0.0).astype(jnp.float32)
    right_inside = jnp.where(has_right, 1.0, 0.0).astype(jnp.float32)

    def inside(r):
        if r < REACH:
            return left_inside
        if r >= REACH + rows:
            return right_inside
        return 1.0

    pl.semaphore_wait(barrier, n - 1 + slabs - 1)

    def halo(ref, send, recv, t):
        at = pl.ds(pl.multiple_of(TILE * t + TILE, TILE), TILE)
        source = ref.at[:, mid, at, :]
        to_left = pltpu.make_async_remote_copy(
            source, ref.at[:, pl.ds(REACH + rows, REACH), at, :], send.at[0, t], recv.at[0, t],
            device_id={"space": lax.rem(s + n - 1, n)}, device_id_type=MESH,
        )
        to_right = pltpu.make_async_remote_copy(
            source, ref.at[:, pl.ds(0, REACH), at, :], send.at[1, t], recv.at[1, t],
            device_id={"space": lax.rem(s + 1, n)}, device_id_type=MESH,
        )
        return to_left, to_right

    def halo_start(ref, send, recv, t):
        to_left, to_right = halo(ref, send, recv, t)
        pl.when(has_left)(to_left.start)
        pl.when(has_right)(to_right.start)

    def halo_arrived(ref, send, recv, t):
        to_left, to_right = halo(ref, send, recv, t)
        pl.when(has_right)(to_left.wait_recv)
        pl.when(has_left)(to_right.wait_recv)

    def halo_sent(ref, send, recv, t):
        to_left, to_right = halo(ref, send, recv, t)
        pl.when(has_left)(to_left.wait_send)
        pl.when(has_right)(to_right.wait_send)

    def over(lo, hi, act):
        def one(t, carry):
            act(t)
            return carry

        lax.fori_loop(lo, hi, one, 0)

    def to_second(t):
        at = pl.ds(pl.multiple_of(TILE * t, TILE), TILE)
        padded = pl.ds(pl.multiple_of(TILE * t + TILE, TILE), TILE)
        return pltpu.make_async_remote_copy(
            x.at[:, :, at, :], e2.at[:, mid, padded, :], x_send.at[t], s_recv.at[t],
            device_id={"tm": lax.rem(p + 2, slabs)}, device_id_type=MESH,
        )

    def to_relaxed(t):
        at = pl.ds(pl.multiple_of(TILE * t, TILE), TILE)
        return pltpu.make_async_remote_copy(
            x.at[:, :, at, :], relaxed.at[:, :, at, :], r_send.at[t], r_recv.at[t],
            device_id={"tm": lax.rem(p + 1, slabs)}, device_id_type=MESH,
        )

    def passed_on(t):
        at = pl.ds(pl.multiple_of(TILE * t, TILE), TILE)
        padded = pl.ds(pl.multiple_of(TILE * t + TILE, TILE), TILE)
        return pltpu.make_async_remote_copy(
            e2.at[:, mid, padded, :], relaxed.at[:, :, at, :], f_send.at[t], r_recv.at[t],
            device_id={"tm": lax.rem(p + slabs - 1, slabs)}, device_id_type=MESH,
        )

    sends_second = p != 2
    sends_relaxed = lax.rem(p, 2) == 0
    passes_on = p == slabs - 1

    pl.when(p < slabs - 1)(own_guess.wait)
    pl.when(p == slabs - 1)(own_start.wait)
    over(0, tiles, functools.partial(halo_start, e1, h1_send, h1_recv))

    def stage_one(k, carry):
        later = (k + CHUNKS - 1) // CHUNKS
        final = (k + 1) // CHUNKS
        ready = 2 * k + 4 - 2 * final
        over((2 * k + 2) * later, ready, functools.partial(halo_arrived, e1, h1_send, h1_recv))
        out_lo, out_hi = 2 * k + later, 2 * k + 3 - final
        phi(e1, x, w1, w2, src, inv, inside, rows, 2 * k, ready, out_lo, out_hi)

        def send(t):
            pl.when(sends_second)(lambda: to_second(t).start())
            pl.when(sends_relaxed)(lambda: to_relaxed(t).start())

        over(out_lo, out_hi, send)
        return carry

    lax.fori_loop(0, CHUNKS, stage_one, 0)

    pl.when(p == 0)(first_start.wait)

    def take(t):
        pl.when(p > 0)(lambda: to_second(t).wait_recv())
        halo_start(e2, h2_send, h2_recv, t)
        pl.when(passes_on)(lambda: passed_on(t).start())

    over(0, 3, take)

    def stage_two(k, carry):
        later = (k + CHUNKS - 1) // CHUNKS
        final = (k + 1) // CHUNKS
        next_final = (k + 2) // CHUNKS - final
        over(2 * k + 3 - final, 2 * k + 5 - next_final - 3 * final, take)
        ready = 2 * k + 3 - final
        over(2 * k + later, ready, functools.partial(halo_arrived, e2, h2_send, h2_recv))
        phi(e2, again, w1, w2, src, inv, inside, rows, 2 * k - later, ready, 2 * k, 2 * k + 2)
        return carry

    lax.fori_loop(0, CHUNKS, stage_two, 0)

    load_guess.wait()
    pl.when(p > 0)(lambda: over(0, tiles, lambda t: to_relaxed(t).wait_recv()))

    @pl.when(p == 0)
    def _():
        def one(t):
            at = pl.ds(pl.multiple_of(TILE * t, TILE), TILE)
            for c in range(comp):
                for r in range(rows):
                    relaxed[c, r, at, :] = again[c, r, at, :]

        over(0, tiles, one)

    def gather(t, totals):
        at = pl.ds(pl.multiple_of(TILE * t, TILE), TILE)
        totals = list(totals)
        for c in range(comp):
            for r in range(rows):
                value = again[c, r, at, :]
                totals[c] = totals[c] + (value - guess[c, r, at, :])
                rest[c, r, at, :] = value - relaxed[c, r, at, :]
        return tuple(totals)

    totals = lax.fori_loop(0, tiles, gather, tuple(border for _ in range(comp)))
    sums[s] = border
    for c in range(comp):
        sums[s, pl.ds(c, 1), :] = jnp.sum(totals[c], axis=0, keepdims=True)

    def share(d):
        return pltpu.make_async_remote_copy(
            sums.at[s], sums.at[s], sum_send.at[d], sum_recv.at[s],
            device_id={"space": lax.rem(s + d, n)}, device_id_type=MESH,
        )

    def shared_arrived(d):
        source = lax.rem(s + d, n)
        pltpu.make_async_remote_copy(
            sums.at[source], sums.at[source], sum_send.at[d], sum_recv.at[source],
            device_id={"space": source}, device_id_type=MESH,
        ).wait_recv()

    over(1, n, lambda d: share(d).start())
    out_rest = pltpu.make_async_copy(rest, residual_ref.at[0], out_sem.at[0])
    out_rest.start()
    over(1, n, shared_arrived)
    total = lax.fori_loop(0, n, lambda i, held: held + sums[i], border)

    lane = lax.broadcasted_iota(jnp.int32, (TILE, nz), 1)
    width = 1
    while width < BLK:
        upper = pltpu.roll(total, nz - width, 1)
        lower = pltpu.roll(total, width, 1)
        total = total + jnp.where((lane // width) % 2 == 0, upper, lower)
        width *= 2
    terms[p] = total * (1.0 / (rows * n * ny * BLK))

    def tell(d):
        return pltpu.make_async_remote_copy(
            terms.at[p], terms.at[p], term_send.at[d], term_recv.at[p],
            device_id={"tm": lax.rem(p + d, slabs)}, device_id_type=MESH,
        )

    for d in range(1, slabs):
        tell(d).start()
    for d in range(1, slabs):
        source = lax.rem(p + d, slabs)
        pltpu.make_async_remote_copy(
            terms.at[source], terms.at[source], term_send.at[d], term_recv.at[source],
            device_id={"tm": source}, device_id_type=MESH,
        ).wait_recv()

    decay = 1.0 / (1.0 + STEPS_SLAB * time_step * linear_rate)
    error = terms[0]
    for j in range(1, slabs):
        error = jnp.where(p >= j, decay * error + terms[j], error)
    spread = [jnp.broadcast_to(error[c : c + 1], (TILE, nz)) for c in range(comp)]

    def correct(t):
        at = pl.ds(pl.multiple_of(TILE * t, TILE), TILE)
        for c in range(comp):
            for r in range(rows):
                result[c, r, at, :] = relaxed[c, r, at, :] + spread[c]

    over(0, tiles, correct)
    out_result = pltpu.make_async_copy(result, corrected_ref.at[0], out_sem.at[1])
    out_result.start()

    def sent(t):
        halo_sent(e1, h1_send, h1_recv, t)
        halo_sent(e2, h2_send, h2_recv, t)
        pl.when(sends_second)(lambda: to_second(t).wait_send())
        pl.when(sends_relaxed)(lambda: to_relaxed(t).wait_send())
        pl.when(passes_on)(lambda: passed_on(t).wait_send())

    over(0, tiles, sent)
    over(1, n, lambda d: share(d).wait_send())
    for d in range(1, slabs):
        tell(d).wait_send()
    out_rest.wait()
    out_result.wait()


def per_device(n, slabs, q_start, guess):
    comp, rows, ny, nz = q_start.shape
    tiles = ny // TILE
    wide = rows + 2 * REACH
    vmem = lambda *shape: pltpu.VMEM(shape, jnp.float32)
    sems = lambda *shape: pltpu.SemaphoreType.DMA(shape)
    padded = (wide, ny + 2 * TILE, nz)
    block = (comp, rows, ny, nz)
    return pl.pallas_call(
        functools.partial(kernel, n, slabs),
        out_shape=(jax.ShapeDtypeStruct(guess.shape, jnp.float32),) * 2,
        in_specs=[pl.BlockSpec(memory_space=pl.ANY)] * 2,
        out_specs=(pl.BlockSpec(memory_space=pl.ANY),) * 2,
        scratch_shapes=[
            vmem(comp, *padded), vmem(comp, *padded), vmem(comp, *padded), vmem(comp, *padded),
            vmem(comp, *padded), vmem(*padded),
            vmem(*block), vmem(*block), vmem(*block), vmem(*block), vmem(*block), vmem(*block),
            vmem(n, TILE, nz), vmem(slabs, TILE, nz),
            sems(3), sems(2, tiles), sems(2, tiles), sems(2, tiles), sems(2, tiles),
            sems(tiles), sems(tiles), sems(tiles), sems(tiles), sems(tiles),
            sems(n), sems(n), sems(slabs), sems(slabs), sems(2),
        ],
        compiler_params=pltpu.CompilerParams(
            collective_id=0, has_side_effects=True, vmem_limit_bytes=32 * 1024 * 1024
        ),
    )(q_start, guess)


def solution(mesh):
    return jax.shard_map(
        functools.partial(per_device, mesh.shape["space"], mesh.shape["tm"]),
        mesh=mesh,
        in_specs=(P(None, "space", None, None), P("tm", None, "space", None, None)),
        out_specs=(P("tm", None, "space", None, None), P("tm", None, "space", None, None)),
        check_vma=False,
    )
```

time: 118 us -> 48.2 us (0.41); the launches traced: 116 us -> 48 us
  Pallas kernels: 0 us -> 43.5 us
  blocking collectives: 38.3 us -> 0 us
  waiting for transfers between devices: 24.6 us -> 0 us
  starting transfers between devices: 22.6 us -> 0 us
  other arithmetic: 17.1 us -> 0 us
  local copies, waits for them, and re-layouts: 12.4 us -> 3.84 us
    pallas_call x0 -> x1, Pallas kernels: none -> 43.5 us  [per_device(): pl.pallas_call(functools.partial(kernel, n, slabs), out_shape=(jax.ShapeD...]
    ppermute x6 -> x0, waiting for transfers between devices: 24.6 us -> none  [the longest x2 23.2 us: passed_along(): return lax.ppermute(block, axis, route)]
    ppermute x6 -> x0, starting transfers between devices: 22.6 us -> none  [the longest x2 11.9 us: with_halo(): lax.ppermute(lax.slice_in_dim(block, block.shape[dim] - width, None, axis...]
    psum x1 -> x0, blocking collectives: 19.4 us -> none  [per_device(): totals = lax.psum(partial_sum, 'space')]
    unnamed x1 -> x0, blocking collectives: 10.8 us -> none
    slice x38 -> x0, local copies, waits for them, and re-layouts: 8.51 us -> none  [the longest x16 6.74 us: jacobi(): along_z = jnp.roll(inner, 1, 3) + jnp.roll(inner, -1, 3)]
    mul x7 -> x0, other arithmetic: 8.34 us -> none  [advance(): current = current * inside[done:done + rows][None, :, None, None]]
    all_gather x1 -> x0, blocking collectives: 8.09 us -> none  [prefix(): gathered = jax.tree.map(lambda a: lax.all_gather(a, axis), part)]
  transfers between devices with their start and end apart: 6 -> 0, of which waited for: 3 -> 0; matrix products, arithmetic and copies ran while one was open for 1% -> 0% of each run, Pallas kernels for 0% -> 0%
where the time goes in v1:
time: 48.2 us; the launch traced here: 48 us
  Pallas kernels  43.5 us (90%)
  local copies, waits for them, and re-layouts  3.84 us (8%)
  between operations  0.65 us (1%)
    pallas_call x1, Pallas kernels, per_device(): pl.pallas_call(functools.partial(kernel, n, slabs), out_shape=(jax.ShapeD...  43.5 us
    unnamed x6, local copies, waits for them, and re-layouts  3.84 us

profile of v1, /device:TPU:0, one launch (start us, length us, event | category | flops | bytes accessed | tf_op | source)
XLA Modules:
  0.0 48.0 jit_solution(856090341544503611)
XLA Ops:
  0.6 0.0 copy-start
  0.6 1.1 %copy-done = f32[5,4,64,128]{3,2,1,0:T(8,128)S(1)} copy-done((f32[5,4,64,128]{3,2,1,0:T(8,128)S(1)}, f32[5,4,64,128]{3,2,1,0:T(8,128)}, u32[]{:S(2)}) %copy-start) | copy-done | bytes 655384
  1.7 0.0 copy-start.1
  1.7 1.1 %copy-done.1 = f32[1,5,4,64,128]{4,3,2,1,0:T(8,128)S(1)} copy-done((f32[1,5,4,64,128]{4,3,2,1,0:T(8,128)S(1)}, f32[1,5,4,64,128]{4,3,2,1,0:T(8,128)}, u32[]{:S(2)}) %copy-start.1) | copy-done | bytes 655384
  2.8 43.5 %shard_map.41 = (f32[1,5,4,64,128]{4,3,2,1,0:T(8,128)S(1)}, f32[1,5,4,64,128]{4,3,2,1,0:T(8,128)S(1)}) custom-call(f32[5,4,64,128]{3,2,1,0:T(8,128)S(1)} %copy-done, f32[1,5,4,64,128]{4,3,2,1,0:T(8,128)S(1)} %copy-done.1), custom_call_target="tpu_custom_call" | custom-call | tf_op jit(solution)/shard_map/pallas_call | solution.py:411
  46.3 0.8 %copy.6 = f32[1,5,4,64,128]{4,3,2,1,0:T(8,128)} copy(f32[1,5,4,64,128]{4,3,2,1,0:T(8,128)S(1)} %get-tuple-element.4) | data formatting | bytes 1310720
  47.2 0.8 %copy.7 = f32[1,5,4,64,128]{4,3,2,1,0:T(8,128)} copy(f32[1,5,4,64,128]{4,3,2,1,0:T(8,128)S(1)} %get-tuple-element.5) | data formatting | bytes 1310720
Async XLA Ops:
  0.6 1.1 %copy-start = (f32[5,4,64,128]{3,2,1,0:T(8,128)S(1)}, f32[5,4,64,128]{3,2,1,0:T(8,128)}, u32[]{:S(2)}) copy-start(f32[5,4,64,128]{3,2,1,0:T(8,128)} %q_ref.1) | copy-start | bytes 1966084
  1.7 1.1 %copy-start.1 = (f32[1,5,4,64,128]{4,3,2,1,0:T(8,128)S(1)}, f32[1,5,4,64,128]{4,3,2,1,0:T(8,128)}, u32[]{:S(2)}) copy-start(f32[1,5,4,64,128]{4,3,2,1,0:T(8,128)} %g_ref.1) | copy-start | bytes 1966084

commit v2 on v1

--- a/solution.py
+++ b/solution.py
@@ -123,8 +123,8 @@
 
 
 def kernel(
-    n, slabs, q_ref, g_ref, corrected_ref, residual_ref,
-    e1, e2, w1, w2, src, inv, x, again, relaxed, guess, result, rest, sums, terms,
+    n, slabs, q_ref, g_ref, relaxed_ref, again_ref, error_ref,
+    e1, e2, w1, w2, src, inv, x, again, relaxed, guess, sums, terms,
     load_sem, h1_send, h1_recv, h2_send, h2_recv, x_send, r_send, f_send, s_recv, r_recv,
     sum_send, sum_recv, term_send, term_recv, out_sem,
 ):
@@ -136,6 +136,16 @@
     body = pl.ds(TILE, ny)
     has_left, has_right = s > 0, s < n - 1
 
+    barrier = pltpu.get_barrier_semaphore()
+
+    def greet_space(d, carry):
+        pl.semaphore_signal(barrier, inc=1, device_id={"space": lax.rem(s + d, n)}, device_id_type=MESH)
+        return carry
+
+    lax.fori_loop(1, n, greet_space, 0)
+    for d in range(1, slabs):
+        pl.semaphore_signal(barrier, inc=1, device_id={"tm": lax.rem(p + d, slabs)}, device_id_type=MESH)
+
     own = e1.at[:, mid, body, :]
     load_guess = pltpu.make_async_copy(g_ref.at[0], guess, load_sem.at[0])
     load_guess.start()
@@ -146,16 +156,6 @@
     pl.when(p == slabs - 1)(own_start.start)
     pl.when(p == 0)(first_start.start)
 
-    barrier = pltpu.get_barrier_semaphore()
-
-    def greet_space(d, carry):
-        pl.semaphore_signal(barrier, inc=1, device_id={"space": lax.rem(s + d, n)}, device_id_type=MESH)
-        return carry
-
-    lax.fori_loop(1, n, greet_space, 0)
-    for d in range(1, slabs):
-        pl.semaphore_signal(barrier, inc=1, device_id={"tm": lax.rem(p + d, slabs)}, device_id_type=MESH)
-
     wide = rows + 2 * REACH
     border = jnp.zeros((TILE, nz), jnp.float32)
 
@@ -261,12 +261,12 @@
     over(0, tiles, functools.partial(halo_start, e1, h1_send, h1_recv))
 
     def stage_one(k, carry):
-        later = (k + CHUNKS - 1) // CHUNKS
-        final = (k + 1) // CHUNKS
-        ready = 2 * k + 4 - 2 * final
-        over((2 * k + 2) * later, ready, functools.partial(halo_arrived, e1, h1_send, h1_recv))
-        out_lo, out_hi = 2 * k + later, 2 * k + 3 - final
-        phi(e1, x, w1, w2, src, inv, inside, rows, 2 * k, ready, out_lo, out_hi)
+        later = (k + CHUNKS) // (CHUNKS + 1)
+        final = k // CHUNKS
+        ready = 2 * k + 2 - 2 * final
+        over(2 * k * later, ready, functools.partial(halo_arrived, e1, h1_send, h1_recv))
+        out_lo, out_hi = 2 * k - later, 2 * k + 1 - final
+        phi(e1, x, w1, w2, src, inv, inside, rows, 2 * k - 2 * later, ready, out_lo, out_hi)
 
         def send(t):
             pl.when(sends_second)(lambda: to_second(t).start())
@@ -275,7 +275,7 @@
         over(out_lo, out_hi, send)
         return carry
 
-    lax.fori_loop(0, CHUNKS, stage_one, 0)
+    lax.fori_loop(0, CHUNKS + 1, stage_one, 0)
 
     pl.when(p == 0)(first_start.wait)
 
@@ -286,7 +286,7 @@
 
     over(0, 3, take)
 
-    def stage_two(k, carry):
+    def stage_two(k, totals):
         later = (k + CHUNKS - 1) // CHUNKS
         final = (k + 1) // CHUNKS
         next_final = (k + 2) // CHUNKS - final
@@ -294,34 +294,17 @@
         ready = 2 * k + 3 - final
         over(2 * k + later, ready, functools.partial(halo_arrived, e2, h2_send, h2_recv))
         phi(e2, again, w1, w2, src, inv, inside, rows, 2 * k - later, ready, 2 * k, 2 * k + 2)
-        return carry
-
-    lax.fori_loop(0, CHUNKS, stage_two, 0)
-
-    load_guess.wait()
-    pl.when(p > 0)(lambda: over(0, tiles, lambda t: to_relaxed(t).wait_recv()))
-
-    @pl.when(p == 0)
-    def _():
-        def one(t):
-            at = pl.ds(pl.multiple_of(TILE * t, TILE), TILE)
-            for c in range(comp):
-                for r in range(rows):
-                    relaxed[c, r, at, :] = again[c, r, at, :]
-
-        over(0, tiles, one)
+        return lax.fori_loop(2 * k, 2 * k + 2, gather, totals)
 
     def gather(t, totals):
         at = pl.ds(pl.multiple_of(TILE * t, TILE), TILE)
-        totals = list(totals)
-        for c in range(comp):
-            for r in range(rows):
-                value = again[c, r, at, :]
-                totals[c] = totals[c] + (value - guess[c, r, at, :])
-                rest[c, r, at, :] = value - relaxed[c, r, at, :]
-        return tuple(totals)
-
-    totals = lax.fori_loop(0, tiles, gather, tuple(border for _ in range(comp)))
+        return tuple(
+            total + sum(again[c, r, at, :] - guess[c, r, at, :] for r in range(rows))
+            for c, total in enumerate(totals)
+        )
+
+    load_guess.wait()
+    totals = lax.fori_loop(0, CHUNKS, stage_two, tuple(border for _ in range(comp)))
     sums[s] = border
     for c in range(comp):
         sums[s, pl.ds(c, 1), :] = jnp.sum(totals[c], axis=0, keepdims=True)
@@ -340,8 +323,13 @@
         ).wait_recv()
 
     over(1, n, lambda d: share(d).start())
-    out_rest = pltpu.make_async_copy(rest, residual_ref.at[0], out_sem.at[0])
-    out_rest.start()
+    out_again = pltpu.make_async_copy(again, again_ref, out_sem.at[0])
+    out_again.start()
+    pl.when(p > 0)(lambda: over(0, tiles, lambda t: to_relaxed(t).wait_recv()))
+    out_first = pltpu.make_async_copy(again, relaxed_ref, out_sem.at[1])
+    out_relaxed = pltpu.make_async_copy(relaxed, relaxed_ref, out_sem.at[1])
+    pl.when(p == 0)(out_first.start)
+    pl.when(p > 0)(out_relaxed.start)
     over(1, n, shared_arrived)
     total = lax.fori_loop(0, n, lambda i, held: held + sums[i], border)
 
@@ -373,17 +361,7 @@
     error = terms[0]
     for j in range(1, slabs):
         error = jnp.where(p >= j, decay * error + terms[j], error)
-    spread = [jnp.broadcast_to(error[c : c + 1], (TILE, nz)) for c in range(comp)]
-
-    def correct(t):
-        at = pl.ds(pl.multiple_of(TILE * t, TILE), TILE)
-        for c in range(comp):
-            for r in range(rows):
-                result[c, r, at, :] = relaxed[c, r, at, :] + spread[c]
-
-    over(0, tiles, correct)
-    out_result = pltpu.make_async_copy(result, corrected_ref.at[0], out_sem.at[1])
-    out_result.start()
+    error_ref[...] = error
 
     def sent(t):
         halo_sent(e1, h1_send, h1_recv, t)
@@ -396,8 +374,9 @@
     over(1, n, lambda d: share(d).wait_send())
     for d in range(1, slabs):
         tell(d).wait_send()
-    out_rest.wait()
-    out_result.wait()
+    out_again.wait()
+    pl.when(p == 0)(out_first.wait)
+    pl.when(p > 0)(out_relaxed.wait)
 
 
 def per_device(n, slabs, q_start, guess):
@@ -408,24 +387,28 @@
     sems = lambda *shape: pltpu.SemaphoreType.DMA(shape)
     padded = (wide, ny + 2 * TILE, nz)
     block = (comp, rows, ny, nz)
-    return pl.pallas_call(
+    relaxed, again, error = pl.pallas_call(
         functools.partial(kernel, n, slabs),
-        out_shape=(jax.ShapeDtypeStruct(guess.shape, jnp.float32),) * 2,
+        out_shape=(jax.ShapeDtypeStruct(block, jnp.float32),) * 2
+        + (jax.ShapeDtypeStruct((TILE, nz), jnp.float32),),
         in_specs=[pl.BlockSpec(memory_space=pl.ANY)] * 2,
-        out_specs=(pl.BlockSpec(memory_space=pl.ANY),) * 2,
+        out_specs=(pl.BlockSpec(memory_space=pl.ANY),) * 2 + (pl.BlockSpec(memory_space=pltpu.VMEM),),
         scratch_shapes=[
             vmem(comp, *padded), vmem(comp, *padded), vmem(comp, *padded), vmem(comp, *padded),
             vmem(comp, *padded), vmem(*padded),
-            vmem(*block), vmem(*block), vmem(*block), vmem(*block), vmem(*block), vmem(*block),
+            vmem(*block), vmem(*block), vmem(*block), vmem(*block),
             vmem(n, TILE, nz), vmem(slabs, TILE, nz),
             sems(3), sems(2, tiles), sems(2, tiles), sems(2, tiles), sems(2, tiles),
             sems(tiles), sems(tiles), sems(tiles), sems(tiles), sems(tiles),
             sems(n), sems(n), sems(slabs), sems(slabs), sems(2),
         ],
         compiler_params=pltpu.CompilerParams(
-            collective_id=0, has_side_effects=True, vmem_limit_bytes=32 * 1024 * 1024
+            collective_id=0, has_side_effects=True, vmem_limit_bytes=60 * 1024 * 1024
         ),
     )(q_start, guess)
+    corrected = relaxed + error[:comp, None, None, :]
+    residual = again - relaxed
+    return corrected[None], residual[None]
 
 
 def solution(mesh):

time: 48.2 us -> 45.7 us (0.948)
  local copies, waits for them, and re-layouts: 3.84 us -> 0.68 us
  other arithmetic: 0 us -> 2.5 us
  Pallas kernels: 43.5 us -> 41.7 us
    unnamed x6 -> x2, local copies, waits for them, and re-layouts: 3.84 us -> 0.68 us
    broadcast_in_dim x0 -> x1, other arithmetic: none -> 2.5 us  [per_device(): return (corrected[None], residual[None])]
    pallas_call x1, Pallas kernels: 43.5 us -> 41.7 us  [per_device(): pl.pallas_call(functools.partial(kernel, n, slabs), out_shape=(jax.ShapeD...]
where the time goes in v2:
time: 45.7 us; the launch traced here: 45.5 us
  Pallas kernels  41.7 us (91%)
  other arithmetic  2.5 us (5%)
  local copies, waits for them, and re-layouts  0.68 us (1%)
  between operations  0.65 us (1%)
    pallas_call x1, Pallas kernels, per_device(): pl.pallas_call(functools.partial(kernel, n, slabs), out_shape=(jax.ShapeD...  41.7 us
    broadcast_in_dim x1, other arithmetic, per_device(): return (corrected[None], residual[None])  2.5 us

profile of v2, /device:TPU:0, one launch (start us, length us, event | category | flops | bytes accessed | tf_op | source)
XLA Modules:
  0.0 45.5 jit_solution(2740422152104932474)
XLA Ops:
  0.6 41.7 %shard_map.41 = (f32[5,4,64,128]{3,2,1,0:T(8,128)}, f32[5,4,64,128]{3,2,1,0:T(8,128)}, f32[8,128]{1,0:T(8,128)}) custom-call(f32[5,4,64,128]{3,2,1,0:T(8,128)} %q_ref.1, f32[1,5,4,64,128]{4,3,2,1,0:T(8,128)} %g_ref.1), custom_call_target="tpu_custom_call" | custom-call | tf_op jit(solution)/shard_map/pallas_call | solution.py:390
  42.3 0.0 copy-start
  42.4 0.7 %copy-done = f32[8,128]{1,0:T(8,128)S(1)} copy-done((f32[8,128]{1,0:T(8,128)S(1)}, f32[8,128]{1,0:T(8,128)}, u32[]{:S(2)}) %copy-start) | copy-done | bytes 4120
  43.0 2.5 %subtract_bitcast_fusion = (f32[1,5,4,64,128]{4,3,2,1,0:T(8,128)}, f32[1,5,4,64,128]{4,3,2,1,0:T(8,128)}) fusion(f32[5,4,64,128]{3,2,1,0:T(8,128)} %get-tuple-element.7, f32[5,4,64,128]{3,2,1,0:T(8,128)} %get-tuple-element.5, f32[5,128]{1,0:T(8,128)S(1)} %bitcast.5), kind=kLoop, calls=%fused_computation | loop fusion | flops 327680 | bytes 2624000 | tf_op jit(solution)/shard_map/broadcast_in_dim | solution.py:411
Async XLA Ops:
  42.3 0.7 %copy-start = (f32[8,128]{1,0:T(8,128)S(1)}, f32[8,128]{1,0:T(8,128)}, u32[]{:S(2)}) copy-start(f32[8,128]{1,0:T(8,128)} %get-tuple-element.6) | copy-start | bytes 12292

commit v3 on v2

--- a/solution.py
+++ b/solution.py
@@ -20,7 +20,6 @@
 
 REACH = STEPS_SLAB * SWEEPS
 TILE = 8
-CHUNKS = 4
 MESH = pl.DeviceIdType.MESH
 
 
@@ -43,90 +42,82 @@
     return source, diagonal
 
 
-def neighbours(ref, c, r, t, before, now, after, edge=False):
+def neighbours(ref, c, r, t, before, now, after):
     along_x = before + after
-    if edge:
-        higher = pltpu.roll(now, TILE - 1, 0)
-    else:
-        higher = ref[c, r, pl.ds(TILE * t + TILE + 1, TILE), :]
-    along_y = ref[c, r, pl.ds(TILE * t + TILE - 1, TILE), :] + higher
+    along_y = ref[c, r, pl.ds(TILE * t + TILE - 1, TILE), :] + ref[c, r, pl.ds(TILE * t + TILE + 1, TILE), :]
     lanes = now.shape[1]
     along_z = pltpu.roll(now, 1, 1) + pltpu.roll(now, lanes - 1, 1)
     return (cross / axial) * (along_x + along_y) + along_z
 
 
+def padded_at(t):
+    return pl.ds(pl.multiple_of(TILE * t + TILE, TILE), TILE)
+
+
 def tile_rows(ref, r, t):
-    at = pl.ds(pl.multiple_of(TILE * t + TILE, TILE), TILE)
-    return [ref[c, r, at, :] for c in range(ref.shape[0])]
-
-
-def first_sweep(ref, out, src, inv, rows, inside, lo, hi, partial):
-    comp = ref.shape[0]
-    tiles = ref.shape[2] // TILE - 2
-
-    def one(edge, t, carry):
-        at = pl.ds(pl.multiple_of(TILE * t + TILE, TILE), TILE)
-        before, now = tile_rows(ref, rows[0] - 1, t), tile_rows(ref, rows[0], t)
-        for r in rows:
-            after = tile_rows(ref, r + 1, t)
-            source, diagonal = bulk(now)
-            inverse = inside(r) / diagonal
-            scaled = axial * inverse
-            inv[r, at, :] = scaled
-            for c in range(comp):
-                part = source[c] * inverse
-                src[c, r, at, :] = part
-                out[c, r, at, :] = part + scaled * neighbours(
-                    ref, c, r, t, before[c], now[c], after[c], edge
-                )
-            before, now = now, after
-        return carry
-
-    if not partial:
-        lax.fori_loop(lo, hi, functools.partial(one, False), 0)
-        return
-    last = hi - 1 + lax.div(hi, tiles)
-    lax.fori_loop(lo, last, functools.partial(one, False), 0)
-    lax.fori_loop(last, hi, functools.partial(one, True), 0)
-
-
-def next_sweep(ref, store, src, inv, rows, lo, hi):
-    comp = ref.shape[0]
-
-    def one(t, carry):
-        at = pl.ds(pl.multiple_of(TILE * t + TILE, TILE), TILE)
-        before, now = tile_rows(ref, rows[0] - 1, t), tile_rows(ref, rows[0], t)
-        for r in rows:
-            after = tile_rows(ref, r + 1, t)
-            scaled = inv[r, at, :]
-            for c in range(comp):
-                store(c, r, t, src[c, r, at, :] + scaled * neighbours(ref, c, r, t, before[c], now[c], after[c]))
-            before, now = now, after
-        return carry
-
-    lax.fori_loop(lo, hi, one, 0)
-
-
-def phi(ref, out, w1, w2, src, inv, inside, rows, lo, hi, out_lo, out_hi):
+    return [ref[c, r, padded_at(t), :] for c in range(ref.shape[0])]
+
+
+def first_sweep(ref, out, src, inv, rows, inside, t):
+    at = padded_at(t)
+    before, now = tile_rows(ref, rows[0] - 1, t), tile_rows(ref, rows[0], t)
+    for r in rows:
+        after = tile_rows(ref, r + 1, t)
+        source, diagonal = bulk(now)
+        inverse = inside(r) / diagonal
+        scaled = axial * inverse
+        inv[r, at, :] = scaled
+        for c in range(ref.shape[0]):
+            part = source[c] * inverse
+            src[c, r, at, :] = part
+            out[c, r, at, :] = part + scaled * neighbours(ref, c, r, t, before[c], now[c], after[c])
+        before, now = now, after
+
+
+def next_sweep(ref, store, src, inv, rows, t):
+    at = padded_at(t)
+    before, now = tile_rows(ref, rows[0] - 1, t), tile_rows(ref, rows[0], t)
+    for r in rows:
+        after = tile_rows(ref, r + 1, t)
+        scaled = inv[r, at, :]
+        for c in range(ref.shape[0]):
+            store(c, r, t, src[c, r, at, :] + scaled * neighbours(ref, c, r, t, before[c], now[c], after[c]))
+        before, now = now, after
+
+
+def phi(ref, out, w1, w2, w3, src, inv, inside, rows, tiles, arrive, finish, carry):
     wide = rows + 2 * REACH
 
     def keep(c, r, t, value):
-        w2[c, r, pl.ds(pl.multiple_of(TILE * t + TILE, TILE), TILE), :] = value
+        w2[c, r, padded_at(t), :] = value
 
     def last(c, r, t, value):
         out[c, r - REACH, pl.ds(pl.multiple_of(TILE * t, TILE), TILE), :] = value
 
-    first_sweep(ref, w1, src, inv, range(1, wide - 1), inside, lo, hi, True)
-    next_sweep(w1, keep, src, inv, range(2, wide - 2), lo, hi)
-    first_sweep(w2, w1, src, inv, range(3, wide - 3), inside, lo, hi, False)
-    next_sweep(w1, last, src, inv, range(4, wide - 4), out_lo, out_hi)
+    sweeps = (
+        lambda t: first_sweep(ref, w1, src, inv, range(1, wide - 1), inside, t),
+        lambda t: next_sweep(w1, keep, src, inv, range(2, wide - 2), t),
+        lambda t: first_sweep(w2, w3, src, inv, range(3, wide - 3), inside, t),
+        lambda t: next_sweep(w3, last, src, inv, range(4, wide - 4), t),
+    )
+
+    def turn(i, carry):
+        pl.when(i < tiles)(lambda: arrive(i))
+        for lag, sweep in enumerate(sweeps):
+            here = jnp.logical_and(i >= lag + 1, i < tiles + lag + 1)
+            pl.when(here)(functools.partial(sweep, i - lag - 1))
+        low = jnp.where(i < REACH, 0, i - REACH)
+        high = jnp.where(i < REACH, 0, i - REACH + 1)
+        return lax.fori_loop(low, high, finish, carry)
+
+    return lax.fori_loop(0, tiles + REACH, turn, carry)
 
 
 def kernel(
-    n, slabs, q_ref, g_ref, relaxed_ref, again_ref, error_ref,
-    e1, e2, w1, w2, src, inv, x, again, relaxed, guess, sums, terms,
+    n, slabs, q_ref, g_ref, corrected_ref, residual_ref,
+    e1, e2, w1, w2, w3, src, inv, x, again, relaxed, guess, result, rest, sums, terms,
     load_sem, h1_send, h1_recv, h2_send, h2_recv, x_send, r_send, f_send, s_recv, r_recv,
-    sum_send, sum_recv, term_send, term_recv, out_sem,
+    sum_send, sum_recv, term_send, term_recv, rest_sem, out_sem,
 ):
     p = lax.axis_index("tm")
     s = lax.axis_index("space")
@@ -160,7 +151,7 @@
     border = jnp.zeros((TILE, nz), jnp.float32)
 
     def clear_pads(r, carry):
-        for ref in (e1, e2, w1, w2):
+        for ref in (e1, e2, w1, w2, w3):
             for c in range(comp):
                 ref[c, r, pl.ds(0, TILE), :] = border
                 ref[c, r, pl.ds(TILE + ny, TILE), :] = border
@@ -260,22 +251,15 @@
     pl.when(p == slabs - 1)(own_start.wait)
     over(0, tiles, functools.partial(halo_start, e1, h1_send, h1_recv))
 
-    def stage_one(k, carry):
-        later = (k + CHUNKS) // (CHUNKS + 1)
-        final = k // CHUNKS
-        ready = 2 * k + 2 - 2 * final
-        over(2 * k * later, ready, functools.partial(halo_arrived, e1, h1_send, h1_recv))
-        out_lo, out_hi = 2 * k - later, 2 * k + 1 - final
-        phi(e1, x, w1, w2, src, inv, inside, rows, 2 * k - 2 * later, ready, out_lo, out_hi)
-
-        def send(t):
-            pl.when(sends_second)(lambda: to_second(t).start())
-            pl.when(sends_relaxed)(lambda: to_relaxed(t).start())
-
-        over(out_lo, out_hi, send)
+    def send(t, carry):
+        pl.when(sends_second)(lambda: to_second(t).start())
+        pl.when(sends_relaxed)(lambda: to_relaxed(t).start())
         return carry
 
-    lax.fori_loop(0, CHUNKS + 1, stage_one, 0)
+    phi(
+        e1, x, w1, w2, w3, src, inv, inside, rows, tiles,
+        functools.partial(halo_arrived, e1, h1_send, h1_recv), send, 0,
+    )
 
     pl.when(p == 0)(first_start.wait)
 
@@ -284,17 +268,9 @@
         halo_start(e2, h2_send, h2_recv, t)
         pl.when(passes_on)(lambda: passed_on(t).start())
 
-    over(0, 3, take)
-
-    def stage_two(k, totals):
-        later = (k + CHUNKS - 1) // CHUNKS
-        final = (k + 1) // CHUNKS
-        next_final = (k + 2) // CHUNKS - final
-        over(2 * k + 3 - final, 2 * k + 5 - next_final - 3 * final, take)
-        ready = 2 * k + 3 - final
-        over(2 * k + later, ready, functools.partial(halo_arrived, e2, h2_send, h2_recv))
-        phi(e2, again, w1, w2, src, inv, inside, rows, 2 * k - later, ready, 2 * k, 2 * k + 2)
-        return lax.fori_loop(2 * k, 2 * k + 2, gather, totals)
+    def arrive(t):
+        pl.when(t < tiles - 1)(lambda: take(t + 1))
+        halo_arrived(e2, h2_send, h2_recv, t)
 
     def gather(t, totals):
         at = pl.ds(pl.multiple_of(TILE * t, TILE), TILE)
@@ -304,7 +280,11 @@
         )
 
     load_guess.wait()
-    totals = lax.fori_loop(0, CHUNKS, stage_two, tuple(border for _ in range(comp)))
+    take(0)
+    totals = phi(
+        e2, again, w1, w2, w3, src, inv, inside, rows, tiles,
+        arrive, gather, tuple(border for _ in range(comp)),
+    )
     sums[s] = border
     for c in range(comp):
         sums[s, pl.ds(c, 1), :] = jnp.sum(totals[c], axis=0, keepdims=True)
@@ -323,13 +303,23 @@
         ).wait_recv()
 
     over(1, n, lambda d: share(d).start())
-    out_again = pltpu.make_async_copy(again, again_ref, out_sem.at[0])
-    out_again.start()
     pl.when(p > 0)(lambda: over(0, tiles, lambda t: to_relaxed(t).wait_recv()))
-    out_first = pltpu.make_async_copy(again, relaxed_ref, out_sem.at[1])
-    out_relaxed = pltpu.make_async_copy(relaxed, relaxed_ref, out_sem.at[1])
-    pl.when(p == 0)(out_first.start)
-    pl.when(p > 0)(out_relaxed.start)
+
+    @pl.when(p == 0)
+    def _():
+        def same(t):
+            at = pl.ds(pl.multiple_of(TILE * t, TILE), TILE)
+            relaxed[:, :, at, :] = again[:, :, at, :]
+
+        over(0, tiles, same)
+
+    def subtract(t):
+        at = pl.ds(pl.multiple_of(TILE * t, TILE), TILE)
+        rest[:, :, at, :] = again[:, :, at, :] - relaxed[:, :, at, :]
+
+    over(0, tiles, subtract)
+    out_rest = pltpu.make_async_copy(rest, residual_ref.at[0], rest_sem.at[0])
+    out_rest.start()
     over(1, n, shared_arrived)
     total = lax.fori_loop(0, n, lambda i, held: held + sums[i], border)
 
@@ -361,7 +351,20 @@
     error = terms[0]
     for j in range(1, slabs):
         error = jnp.where(p >= j, decay * error + terms[j], error)
-    error_ref[...] = error
+    spread = [jnp.broadcast_to(error[c : c + 1], (TILE, nz)) for c in range(comp)]
+
+    def out_result(t):
+        at = pl.ds(pl.multiple_of(TILE * t, TILE), TILE)
+        return pltpu.make_async_copy(result.at[:, :, at, :], corrected_ref.at[0, :, :, at, :], out_sem.at[t])
+
+    def correct(t):
+        at = pl.ds(pl.multiple_of(TILE * t, TILE), TILE)
+        for c in range(comp):
+            for r in range(rows):
+                result[c, r, at, :] = relaxed[c, r, at, :] + spread[c]
+        out_result(t).start()
+
+    over(0, tiles, correct)
 
     def sent(t):
         halo_sent(e1, h1_send, h1_recv, t)
@@ -374,9 +377,8 @@
     over(1, n, lambda d: share(d).wait_send())
     for d in range(1, slabs):
         tell(d).wait_send()
-    out_again.wait()
-    pl.when(p == 0)(out_first.wait)
-    pl.when(p > 0)(out_relaxed.wait)
+    out_rest.wait()
+    over(0, tiles, lambda t: out_result(t).wait())
 
 
 def per_device(n, slabs, q_start, guess):
@@ -387,28 +389,24 @@
     sems = lambda *shape: pltpu.SemaphoreType.DMA(shape)
     padded = (wide, ny + 2 * TILE, nz)
     block = (comp, rows, ny, nz)
-    relaxed, again, error = pl.pallas_call(
+    return pl.pallas_call(
         functools.partial(kernel, n, slabs),
-        out_shape=(jax.ShapeDtypeStruct(block, jnp.float32),) * 2
-        + (jax.ShapeDtypeStruct((TILE, nz), jnp.float32),),
+        out_shape=(jax.ShapeDtypeStruct(guess.shape, jnp.float32),) * 2,
         in_specs=[pl.BlockSpec(memory_space=pl.ANY)] * 2,
-        out_specs=(pl.BlockSpec(memory_space=pl.ANY),) * 2 + (pl.BlockSpec(memory_space=pltpu.VMEM),),
+        out_specs=(pl.BlockSpec(memory_space=pl.ANY),) * 2,
         scratch_shapes=[
             vmem(comp, *padded), vmem(comp, *padded), vmem(comp, *padded), vmem(comp, *padded),
-            vmem(comp, *padded), vmem(*padded),
-            vmem(*block), vmem(*block), vmem(*block), vmem(*block),
+            vmem(comp, *padded), vmem(comp, *padded), vmem(*padded),
+            vmem(*block), vmem(*block), vmem(*block), vmem(*block), vmem(*block), vmem(*block),
             vmem(n, TILE, nz), vmem(slabs, TILE, nz),
             sems(3), sems(2, tiles), sems(2, tiles), sems(2, tiles), sems(2, tiles),
             sems(tiles), sems(tiles), sems(tiles), sems(tiles), sems(tiles),
-            sems(n), sems(n), sems(slabs), sems(slabs), sems(2),
+            sems(n), sems(n), sems(slabs), sems(slabs), sems(1), sems(tiles),
         ],
         compiler_params=pltpu.CompilerParams(
             collective_id=0, has_side_effects=True, vmem_limit_bytes=60 * 1024 * 1024
         ),
     )(q_start, guess)
-    corrected = relaxed + error[:comp, None, None, :]
-    residual = again - relaxed
-    return corrected[None], residual[None]
 
 
 def solution(mesh):

time: 45.7 us -> 46.8 us (1.024)
  other arithmetic: 2.5 us -> 0 us
  local copies, waits for them, and re-layouts: 0.68 us -> 2.89 us
  Pallas kernels: 41.7 us -> 43.1 us
    broadcast_in_dim x1 -> x0, other arithmetic: 2.5 us -> none  [per_device(): return (corrected[None], residual[None])]
    unnamed x2 -> x4, local copies, waits for them, and re-layouts: 0.68 us -> 2.89 us
    pallas_call x1, Pallas kernels: 41.7 us -> 43.1 us  [per_device(): pl.pallas_call(functools.partial(kernel, n, slabs), out_shape=(jax.ShapeD...]
where the time goes in v3:
time: 46.8 us; the launch traced here: 46.7 us
  Pallas kernels  43.1 us (92%)
  local copies, waits for them, and re-layouts  2.89 us (6%)
  between operations  0.65 us (1%)
    pallas_call x1, Pallas kernels, per_device(): pl.pallas_call(functools.partial(kernel, n, slabs), out_shape=(jax.ShapeD...  43.1 us
    unnamed x4, local copies, waits for them, and re-layouts  2.89 us

profile of v3, /device:TPU:0, one launch (start us, length us, event | category | flops | bytes accessed | tf_op | source)
XLA Modules:
  0.0 46.7 jit_solution(2170834910585959924)
XLA Ops:
  0.6 43.1 %shard_map.41 = (f32[1,5,4,64,128]{4,3,2,1,0:T(8,128)}, f32[1,5,4,64,128]{4,3,2,1,0:T(8,128)}) custom-call(f32[5,4,64,128]{3,2,1,0:T(8,128)} %q_ref.1, f32[1,5,4,64,128]{4,3,2,1,0:T(8,128)} %g_ref.1), custom_call_target="tpu_custom_call" | custom-call | tf_op jit(solution)/shard_map/pallas_call | solution.py:392
  43.8 0.0 copy-start
  43.8 2.0 %copy.6 = f32[1,5,4,64,128]{4,3,2,1,0:T(8,128)} copy(f32[1,5,4,64,128]{4,3,2,1,0:T(8,128)} %get-tuple-element.4) | data formatting | bytes 1310720
  45.8 0.0 copy-done
  45.8 0.8 %copy.7 = f32[1,5,4,64,128]{4,3,2,1,0:T(8,128)} copy(f32[1,5,4,64,128]{4,3,2,1,0:T(8,128)S(1)} %copy-done) | data formatting | bytes 1310720
Async XLA Ops:
  43.8 2.1 %copy-start = (f32[1,5,4,64,128]{4,3,2,1,0:T(8,128)S(1)}, f32[1,5,4,64,128]{4,3,2,1,0:T(8,128)}, u32[]{:S(2)}) copy-start(f32[1,5,4,64,128]{4,3,2,1,0:T(8,128)} %get-tuple-element.5) | copy-start | bytes 1966084

commit v4 on v3

--- a/solution.py
+++ b/solution.py
@@ -85,20 +85,17 @@
         before, now = now, after
 
 
-def phi(ref, out, w1, w2, w3, src, inv, inside, rows, tiles, arrive, finish, carry):
+def phi(ref, store, w1, w2, w3, src, inv, inside, rows, tiles, arrive, finish, carry):
     wide = rows + 2 * REACH
 
     def keep(c, r, t, value):
         w2[c, r, padded_at(t), :] = value
-
-    def last(c, r, t, value):
-        out[c, r - REACH, pl.ds(pl.multiple_of(TILE * t, TILE), TILE), :] = value
 
     sweeps = (
         lambda t: first_sweep(ref, w1, src, inv, range(1, wide - 1), inside, t),
         lambda t: next_sweep(w1, keep, src, inv, range(2, wide - 2), t),
         lambda t: first_sweep(w2, w3, src, inv, range(3, wide - 3), inside, t),
-        lambda t: next_sweep(w3, last, src, inv, range(4, wide - 4), t),
+        lambda t: next_sweep(w3, store, src, inv, range(4, wide - 4), t),
     )
 
     def turn(i, carry):
@@ -115,13 +112,13 @@
 
 def kernel(
     n, slabs, q_ref, g_ref, corrected_ref, residual_ref,
-    e1, e2, w1, w2, w3, src, inv, x, again, relaxed, guess, result, rest, sums, terms,
+    e1, e2, w1, w2, w3, src, inv, x, landed, relaxed, again, guess, result, rest, sums, terms,
     load_sem, h1_send, h1_recv, h2_send, h2_recv, x_send, r_send, f_send, s_recv, r_recv,
     sum_send, sum_recv, term_send, term_recv, rest_sem, out_sem,
 ):
     p = lax.axis_index("tm")
     s = lax.axis_index("space")
-    comp, rows, ny, nz = x.shape
+    comp, rows, ny, nz = guess.shape
     tiles = ny // TILE
     mid = pl.ds(REACH, rows)
     body = pl.ds(TILE, ny)
@@ -221,25 +218,20 @@
         lax.fori_loop(lo, hi, one, 0)
 
     def to_second(t):
-        at = pl.ds(pl.multiple_of(TILE * t, TILE), TILE)
-        padded = pl.ds(pl.multiple_of(TILE * t + TILE, TILE), TILE)
         return pltpu.make_async_remote_copy(
-            x.at[:, :, at, :], e2.at[:, mid, padded, :], x_send.at[t], s_recv.at[t],
+            x.at[t], landed.at[t], x_send.at[t], s_recv.at[t],
             device_id={"tm": lax.rem(p + 2, slabs)}, device_id_type=MESH,
         )
 
     def to_relaxed(t):
-        at = pl.ds(pl.multiple_of(TILE * t, TILE), TILE)
         return pltpu.make_async_remote_copy(
-            x.at[:, :, at, :], relaxed.at[:, :, at, :], r_send.at[t], r_recv.at[t],
+            x.at[t], relaxed.at[t], r_send.at[t], r_recv.at[t],
             device_id={"tm": lax.rem(p + 1, slabs)}, device_id_type=MESH,
         )
 
     def passed_on(t):
-        at = pl.ds(pl.multiple_of(TILE * t, TILE), TILE)
-        padded = pl.ds(pl.multiple_of(TILE * t + TILE, TILE), TILE)
         return pltpu.make_async_remote_copy(
-            e2.at[:, mid, padded, :], relaxed.at[:, :, at, :], f_send.at[t], r_recv.at[t],
+            landed.at[t], relaxed.at[t], f_send.at[t], r_recv.at[t],
             device_id={"tm": lax.rem(p + slabs - 1, slabs)}, device_id_type=MESH,
         )
 
@@ -256,15 +248,25 @@
         pl.when(sends_relaxed)(lambda: to_relaxed(t).start())
         return carry
 
+    def to_x(c, r, t, value):
+        x[t, c, r - REACH] = value
+
+    def to_again(c, r, t, value):
+        again[c, r - REACH, pl.ds(pl.multiple_of(TILE * t, TILE), TILE), :] = value
+
     phi(
-        e1, x, w1, w2, w3, src, inv, inside, rows, tiles,
+        e1, to_x, w1, w2, w3, src, inv, inside, rows, tiles,
         functools.partial(halo_arrived, e1, h1_send, h1_recv), send, 0,
     )
 
     pl.when(p == 0)(first_start.wait)
 
     def take(t):
-        pl.when(p > 0)(lambda: to_second(t).wait_recv())
+        @pl.when(p > 0)
+        def _():
+            to_second(t).wait_recv()
+            e2[:, REACH : REACH + rows, padded_at(t), :] = landed[t]
+
         halo_start(e2, h2_send, h2_recv, t)
         pl.when(passes_on)(lambda: passed_on(t).start())
 
@@ -282,7 +284,7 @@
     load_guess.wait()
     take(0)
     totals = phi(
-        e2, again, w1, w2, w3, src, inv, inside, rows, tiles,
+        e2, to_again, w1, w2, w3, src, inv, inside, rows, tiles,
         arrive, gather, tuple(border for _ in range(comp)),
     )
     sums[s] = border
@@ -309,13 +311,13 @@
     def _():
         def same(t):
             at = pl.ds(pl.multiple_of(TILE * t, TILE), TILE)
-            relaxed[:, :, at, :] = again[:, :, at, :]
+            relaxed[t] = again[:, :, at, :]
 
         over(0, tiles, same)
 
     def subtract(t):
         at = pl.ds(pl.multiple_of(TILE * t, TILE), TILE)
-        rest[:, :, at, :] = again[:, :, at, :] - relaxed[:, :, at, :]
+        rest[:, :, at, :] = again[:, :, at, :] - relaxed[t]
 
     over(0, tiles, subtract)
     out_rest = pltpu.make_async_copy(rest, residual_ref.at[0], rest_sem.at[0])
@@ -361,7 +363,7 @@
         at = pl.ds(pl.multiple_of(TILE * t, TILE), TILE)
         for c in range(comp):
             for r in range(rows):
-                result[c, r, at, :] = relaxed[c, r, at, :] + spread[c]
+                result[c, r, at, :] = relaxed[t, c, r] + spread[c]
         out_result(t).start()
 
     over(0, tiles, correct)
@@ -389,22 +391,23 @@
     sems = lambda *shape: pltpu.SemaphoreType.DMA(shape)
     padded = (wide, ny + 2 * TILE, nz)
     block = (comp, rows, ny, nz)
+    tiled = (tiles, comp, rows, TILE, nz)
     return pl.pallas_call(
         functools.partial(kernel, n, slabs),
         out_shape=(jax.ShapeDtypeStruct(guess.shape, jnp.float32),) * 2,
-        in_specs=[pl.BlockSpec(memory_space=pl.ANY)] * 2,
+        in_specs=[pl.BlockSpec(memory_space=pltpu.HBM)] * 2,
         out_specs=(pl.BlockSpec(memory_space=pl.ANY),) * 2,
         scratch_shapes=[
             vmem(comp, *padded), vmem(comp, *padded), vmem(comp, *padded), vmem(comp, *padded),
             vmem(comp, *padded), vmem(comp, *padded), vmem(*padded),
-            vmem(*block), vmem(*block), vmem(*block), vmem(*block), vmem(*block), vmem(*block),
+            vmem(*tiled), vmem(*tiled), vmem(*tiled), vmem(*block), vmem(*block), vmem(*block), vmem(*block),
             vmem(n, TILE, nz), vmem(slabs, TILE, nz),
             sems(3), sems(2, tiles), sems(2, tiles), sems(2, tiles), sems(2, tiles),
             sems(tiles), sems(tiles), sems(tiles), sems(tiles), sems(tiles),
             sems(n), sems(n), sems(slabs), sems(slabs), sems(1), sems(tiles),
         ],
         compiler_params=pltpu.CompilerParams(
-            collective_id=0, has_side_effects=True, vmem_limit_bytes=60 * 1024 * 1024
+            collective_id=0, has_side_effects=True, vmem_limit_bytes=32 * 1024 * 1024
         ),
     )(q_start, guess)
 

time: 46.8 us -> 47.2 us (level)
  local copies, waits for them, and re-layouts: 2.89 us -> 3.84 us
  Pallas kernels: 43.1 us -> 42.6 us
    unnamed x4 -> x6, local copies, waits for them, and re-layouts: 2.89 us -> 3.84 us
    pallas_call x1, Pallas kernels: 43.1 us -> 42.6 us  [per_device(): pl.pallas_call(functools.partial(kernel, n, slabs), out_shape=(jax.ShapeD...]
where the time goes in v4:
time: 47.2 us; the launch traced here: 47 us
  Pallas kernels  42.6 us (90%)
  local copies, waits for them, and re-layouts  3.84 us (8%)
  between operations  0.65 us (1%)
    pallas_call x1, Pallas kernels, per_device(): pl.pallas_call(functools.partial(kernel, n, slabs), out_shape=(jax.ShapeD...  42.6 us
    unnamed x6, local copies, waits for them, and re-layouts  3.84 us

profile of v4, /device:TPU:0, one launch (start us, length us, event | category | flops | bytes accessed | tf_op | source)
XLA Modules:
  0.0 47.0 jit_solution(4502747310964073967)
XLA Ops:
  0.6 0.0 copy-start
  0.6 1.1 %copy-done = f32[5,4,64,128]{3,2,1,0:T(8,128)S(1)} copy-done((f32[5,4,64,128]{3,2,1,0:T(8,128)S(1)}, f32[5,4,64,128]{3,2,1,0:T(8,128)}, u32[]{:S(2)}) %copy-start) | copy-done | bytes 655384
  1.7 0.0 copy-start.1
  1.7 1.1 %copy-done.1 = f32[1,5,4,64,128]{4,3,2,1,0:T(8,128)S(1)} copy-done((f32[1,5,4,64,128]{4,3,2,1,0:T(8,128)S(1)}, f32[1,5,4,64,128]{4,3,2,1,0:T(8,128)}, u32[]{:S(2)}) %copy-start.1) | copy-done | bytes 655384
  2.8 42.6 %shard_map.41 = (f32[1,5,4,64,128]{4,3,2,1,0:T(8,128)S(1)}, f32[1,5,4,64,128]{4,3,2,1,0:T(8,128)S(1)}) custom-call(f32[5,4,64,128]{3,2,1,0:T(8,128)S(1)} %copy-done, f32[1,5,4,64,128]{4,3,2,1,0:T(8,128)S(1)} %copy-done.1), custom_call_target="tpu_custom_call" | custom-call | tf_op jit(solution)/shard_map/pallas_call | solution.py:395
  45.4 0.8 %copy.6 = f32[1,5,4,64,128]{4,3,2,1,0:T(8,128)} copy(f32[1,5,4,64,128]{4,3,2,1,0:T(8,128)S(1)} %get-tuple-element.4) | data formatting | bytes 1310720
  46.2 0.8 %copy.7 = f32[1,5,4,64,128]{4,3,2,1,0:T(8,128)} copy(f32[1,5,4,64,128]{4,3,2,1,0:T(8,128)S(1)} %get-tuple-element.5) | data formatting | bytes 1310720
Async XLA Ops:
  0.6 1.1 %copy-start = (f32[5,4,64,128]{3,2,1,0:T(8,128)S(1)}, f32[5,4,64,128]{3,2,1,0:T(8,128)}, u32[]{:S(2)}) copy-start(f32[5,4,64,128]{3,2,1,0:T(8,128)} %q_ref.1) | copy-start | bytes 1966084
  1.7 1.1 %copy-start.1 = (f32[1,5,4,64,128]{4,3,2,1,0:T(8,128)S(1)}, f32[1,5,4,64,128]{4,3,2,1,0:T(8,128)}, u32[]{:S(2)}) copy-start(f32[1,5,4,64,128]{4,3,2,1,0:T(8,128)} %g_ref.1) | copy-start | bytes 1966084

commit v5 on v4

--- a/solution.py
+++ b/solution.py
@@ -20,6 +20,7 @@
 
 REACH = STEPS_SLAB * SWEEPS
 TILE = 8
+AHEAD = 4
 MESH = pl.DeviceIdType.MESH
 
 
@@ -243,22 +244,6 @@
     pl.when(p == slabs - 1)(own_start.wait)
     over(0, tiles, functools.partial(halo_start, e1, h1_send, h1_recv))
 
-    def send(t, carry):
-        pl.when(sends_second)(lambda: to_second(t).start())
-        pl.when(sends_relaxed)(lambda: to_relaxed(t).start())
-        return carry
-
-    def to_x(c, r, t, value):
-        x[t, c, r - REACH] = value
-
-    def to_again(c, r, t, value):
-        again[c, r - REACH, pl.ds(pl.multiple_of(TILE * t, TILE), TILE), :] = value
-
-    phi(
-        e1, to_x, w1, w2, w3, src, inv, inside, rows, tiles,
-        functools.partial(halo_arrived, e1, h1_send, h1_recv), send, 0,
-    )
-
     pl.when(p == 0)(first_start.wait)
 
     def take(t):
@@ -270,8 +255,25 @@
         halo_start(e2, h2_send, h2_recv, t)
         pl.when(passes_on)(lambda: passed_on(t).start())
 
+    def send(t, carry):
+        pl.when(sends_second)(lambda: to_second(t).start())
+        pl.when(sends_relaxed)(lambda: to_relaxed(t).start())
+        pl.when(t >= AHEAD)(lambda: take(t - AHEAD))
+        return carry
+
+    def to_x(c, r, t, value):
+        x[t, c, r - REACH] = value
+
+    def to_again(c, r, t, value):
+        again[c, r - REACH, pl.ds(pl.multiple_of(TILE * t, TILE), TILE), :] = value
+
+    phi(
+        e1, to_x, w1, w2, w3, src, inv, inside, rows, tiles,
+        functools.partial(halo_arrived, e1, h1_send, h1_recv), send, 0,
+    )
+
     def arrive(t):
-        pl.when(t < tiles - 1)(lambda: take(t + 1))
+        pl.when(jnp.logical_and(t >= tiles - AHEAD - 1, t < tiles - 1))(lambda: take(t + 1))
         halo_arrived(e2, h2_send, h2_recv, t)
 
     def gather(t, totals):
@@ -282,7 +284,6 @@
         )
 
     load_guess.wait()
-    take(0)
     totals = phi(
         e2, to_again, w1, w2, w3, src, inv, inside, rows, tiles,
         arrive, gather, tuple(border for _ in range(comp)),
@@ -407,7 +408,7 @@
             sems(n), sems(n), sems(slabs), sems(slabs), sems(1), sems(tiles),
         ],
         compiler_params=pltpu.CompilerParams(
-            collective_id=0, has_side_effects=True, vmem_limit_bytes=32 * 1024 * 1024
+            collective_id=0, has_side_effects=True, vmem_limit_bytes=53 * 1024 * 1024
         ),
     )(q_start, guess)
 

time: 47.2 us -> 45.7 us (0.968)
  local copies, waits for them, and re-layouts: 3.84 us -> 2.15 us
    unnamed x6 -> x4, local copies, waits for them, and re-layouts: 3.84 us -> 2.15 us
where the time goes in v5:
time: 45.7 us; the launch traced here: 45.5 us
  Pallas kernels  42.7 us (93%)
  local copies, waits for them, and re-layouts  2.15 us (5%)
  between operations  0.65 us (1%)
    pallas_call x1, Pallas kernels, per_device(): pl.pallas_call(functools.partial(kernel, n, slabs), out_shape=(jax.ShapeD...  42.7 us
    unnamed x4, local copies, waits for them, and re-layouts  2.15 us

profile of v5, /device:TPU:0, one launch (start us, length us, event | category | flops | bytes accessed | tf_op | source)
XLA Modules:
  0.0 45.5 jit_solution(1299113618924279832)
XLA Ops:
  0.6 42.7 %shard_map.41 = (f32[1,5,4,64,128]{4,3,2,1,0:T(8,128)S(1)}, f32[1,5,4,64,128]{4,3,2,1,0:T(8,128)}) custom-call(f32[5,4,64,128]{3,2,1,0:T(8,128)} %q_ref.1, f32[1,5,4,64,128]{4,3,2,1,0:T(8,128)} %g_ref.1), custom_call_target="tpu_custom_call" | custom-call | tf_op jit(solution)/shard_map/pallas_call | solution.py:396
  43.3 0.0 copy-start
  43.4 0.8 %copy.6 = f32[1,5,4,64,128]{4,3,2,1,0:T(8,128)} copy(f32[1,5,4,64,128]{4,3,2,1,0:T(8,128)S(1)} %get-tuple-element.4) | data formatting | bytes 1310720
  44.2 0.5 %copy-done = f32[1,5,4,64,128]{4,3,2,1,0:T(8,128)S(1)} copy-done((f32[1,5,4,64,128]{4,3,2,1,0:T(8,128)S(1)}, f32[1,5,4,64,128]{4,3,2,1,0:T(8,128)}, u32[]{:S(2)}) %copy-start) | copy-done | bytes 655384
  44.7 0.8 %copy.7 = f32[1,5,4,64,128]{4,3,2,1,0:T(8,128)} copy(f32[1,5,4,64,128]{4,3,2,1,0:T(8,128)S(1)} %copy-done) | data formatting | bytes 1310720
Async XLA Ops:
  43.3 1.3 %copy-start = (f32[1,5,4,64,128]{4,3,2,1,0:T(8,128)S(1)}, f32[1,5,4,64,128]{4,3,2,1,0:T(8,128)}, u32[]{:S(2)}) copy-start(f32[1,5,4,64,128]{4,3,2,1,0:T(8,128)} %get-tuple-element.5) | copy-start | bytes 1966084
